TPU v7x, 512 devices: a whole 4x4x16 slice. The times are simulated.
512 devices in a mesh: dp: 8 (over y, x_hi), expert: 64 (over z, x_lo, core).
Axes of the slice: x: 4 (x_hi: 2, x_lo: 2; x = x_hi * 2 + x_lo), y: 4, z: 16, core: 2. Of those that a mesh axis runs over, the one named last changes fastest.
Arguments:
- tokens: bfloat16 [65536, 2048], P(('dp', 'expert')), may hold values from -6 to 6
- expert_ids: int32 [65536, 8], P(('dp', 'expert')), may hold values from 0 to 63, all different within a row; in each aligned block of 128 rows (0 to 127, 128 to 255, ...) at most 18 rows name the same one
- keep_mask: int32 [65536, 8], P(('dp', 'expert')), may hold values 0 or 1
- gate_weights: bfloat16 [65536, 8], P(('dp', 'expert')), may hold values from 0.049804688 to 0.5
- hidden_grad: bfloat16 [8, 64, 1152, 384], P('dp', 'expert'), may hold values from -4 to 4
- gate_pre: bfloat16 [8, 64, 1152, 384], P('dp', 'expert'), may hold values from -8 to 8
- up_pre: bfloat16 [8, 64, 1152, 384], P('dp', 'expert'), may hold values from -6 to 6
- gate_proj: bfloat16 [64, 2048, 384], P('expert', 'dp'), may hold values from -0.3125 to 0.3125
- up_proj: bfloat16 [64, 2048, 384], P('expert', 'dp'), may hold values from -0.3125 to 0.3125
Outputs:
- token_grad: bfloat16 [65536, 2048], P(('dp', 'expert'))
- gate_proj_grad: bfloat16 [64, 2048, 384], P('expert', 'dp')
- up_proj_grad: bfloat16 [64, 2048, 384], P('expert', 'dp')
Inputs may be any that keep to these rules, and one draw needn't show every extreme that they name: `expert_ids`: among the 8 experts of one token none repeats; among the pairs of the 128 tokens of one device no expert is named more than 18 times, a bound that some block reaches.
All inputs are finite; a program needn't handle non-finite values. No bound on the sum of `keep_mask` on one device may be relied on, other than what follows from the above.
Results may differ from a plain program's by a relative error of at most 0.015.
Values may be sent and summed in bfloat16 or wider, within the bound.
A program may use at most 128 MiB of HBM per device.

v0:
```python
import jax
import jax.numpy as jnp
from jax import lax
from jax.sharding import PartitionSpec as P


def on_device(
    tokens, expert_ids, keep_mask, gate_weights, hidden_grad, gate_pre, up_pre, gate_proj, up_proj
):
    tok_rows, width = tokens.shape
    topk = expert_ids.shape[1]
    num_dev = lax.axis_size("expert")
    local = gate_proj.shape[0]
    experts_all = num_dev * local
    slot_rows = hidden_grad.shape[2]
    capacity = slot_rows // num_dev
    entries = tok_rows * topk
    route_ids = expert_ids.reshape(-1)
    kept = keep_mask.reshape(-1)
    onehot = (route_ids[:, None] == jnp.arange(experts_all, dtype=jnp.int32)[None, :]).astype(
        jnp.int32
    ) * kept[:, None]
    before = jnp.cumsum(onehot, axis=0) - onehot
    slot = jnp.sum(before * onehot, axis=1)
    target = jnp.where(kept > 0, route_ids * capacity + slot, experts_all * capacity)
    owner = (
        jnp.full((experts_all * capacity,), entries, jnp.int32)
        .at[target]
        .set(jnp.arange(entries, dtype=jnp.int32), mode="drop")
    )
    padded_rows = jnp.concatenate([tokens, jnp.zeros((1, width), jnp.bfloat16)], axis=0)
    send_rows = padded_rows[owner // topk].reshape(num_dev, local * capacity, width)
    padded_weights = jnp.concatenate([gate_weights.reshape(-1), jnp.zeros((1,), jnp.bfloat16)])
    send_weights = padded_weights[owner].reshape(num_dev, local * capacity)
    recv_rows, recv_weights = (
        lax.all_to_all(send_rows, "expert", split_axis=0, concat_axis=0, tiled=True),
        lax.all_to_all(send_weights, "expert", split_axis=0, concat_axis=0, tiled=True),
    )
    inputs_rx = (
        recv_rows.reshape(num_dev, local, capacity, width)
        .transpose(1, 0, 2, 3)
        .reshape(local, slot_rows, width)
    )
    gates_rx = (
        recv_weights.reshape(num_dev, local, capacity).transpose(1, 0, 2).reshape(local, slot_rows)
    )
    pre_a = gate_pre[0].astype(jnp.float32)
    pre_b = up_pre[0].astype(jnp.float32)
    sigmoid_a = 1.0 / (1.0 + jnp.exp(-pre_a))
    scaled = gates_rx.astype(jnp.float32)[:, :, None] * hidden_grad[0].astype(jnp.float32)
    gate_delta = (scaled * pre_b * sigmoid_a * (1.0 + pre_a * (1.0 - sigmoid_a))).astype(
        jnp.bfloat16
    )
    up_delta = (scaled * pre_a * sigmoid_a).astype(jnp.bfloat16)
    part_gate = jnp.einsum(
        "erd,erf->edf", inputs_rx, gate_delta, preferred_element_type=jnp.float32
    ).astype(jnp.bfloat16)
    part_up = jnp.einsum(
        "erd,erf->edf", inputs_rx, up_delta, preferred_element_type=jnp.float32
    ).astype(jnp.bfloat16)
    summed_gate = lax.psum_scatter(part_gate, "dp", scatter_dimension=1, tiled=True).astype(
        jnp.float32
    )
    summed_up = lax.psum_scatter(part_up, "dp", scatter_dimension=1, tiled=True).astype(jnp.float32)
    grad_gate = summed_gate.astype(jnp.bfloat16)
    grad_up = summed_up.astype(jnp.bfloat16)
    stacked = jnp.stack([gate_proj, up_proj], axis=1)
    piece = lax.all_gather(stacked, "dp", axis=2, tiled=True)
    first = jnp.einsum("erf,edf->erd", gate_delta, piece[:, 0], preferred_element_type=jnp.float32)
    second = jnp.einsum("erf,edf->erd", up_delta, piece[:, 1], preferred_element_type=jnp.float32)
    slot_grad = (first + second).astype(jnp.bfloat16)
    outgoing = (
        slot_grad.reshape(local, num_dev, capacity, width)
        .transpose(1, 0, 2, 3)
        .reshape(num_dev, local * capacity, width)
    )
    incoming = lax.all_to_all(outgoing, "expert", split_axis=0, concat_axis=0, tiled=True)
    padded_grad = jnp.concatenate(
        [incoming.reshape(experts_all * capacity, width), jnp.zeros((1, width), jnp.bfloat16)],
        axis=0,
    )
    picked = padded_grad[target].reshape(tok_rows, topk, width)
    token_grad = jnp.sum(picked, axis=1, dtype=jnp.float32).astype(jnp.bfloat16)
    return (token_grad, grad_gate, grad_up)


def solution(mesh):
    return jax.shard_map(
        on_device,
        mesh=mesh,
        in_specs=(
            P(("dp", "expert"), None),
            P(("dp", "expert"), None),
            P(("dp", "expert"), None),
            P(("dp", "expert"), None),
            P("dp", "expert", None, None),
            P("dp", "expert", None, None),
            P("dp", "expert", None, None),
            P("expert", "dp", None),
            P("expert", "dp", None),
        ),
        out_specs=(P(("dp", "expert"), None), P("expert", "dp", None), P("expert", "dp", None)),
        check_vma=False,
    )
```

profile of v0, /device:TPU:1, one launch (start us, length us, event | category | flops | bytes accessed | tf_op | source)
XLA Modules:
  0.0 684.8 jit_solution(16680178439814803371)
XLA Ops:
  7.2 0.7 broadcast_multiply_fusion
  7.9 0.8 copy.24
  8.6 0.1 eq.29
  8.7 0.1 eq.25
  8.8 0.7 broadcast_compare_fusion
  9.5 0.8 copy.25
  10.3 0.1 mul.235
  10.4 0.1 mul.232
  10.5 0.1 copy.22
  10.6 0.1 gt.18
  10.7 0.8 copy.21
  11.5 0.1 reshape.380
  11.6 0.1 copy.23
  11.7 0.1 mul.231
  11.9 18.0 %reduce-window.6 = s32[64,8,128]{2,1,0:T(8,128)S(1)} reduce-window(s32[64,8,128]{2,1,0:T(8,128)S(1)} %fusion.18, s32[]{:T(128)} %constant.12.clone.1), window={size=1x1x128 pad=0_0x0_0x127_0}, to_apply=%region_0.0 | reduce-window | flops 8323072 | bytes 524292 | tf_op jit(solution)/shard_map/reduce-window
  29.9 0.1 slice.22
  30.0 0.1 copy.26
  30.2 0.1 copy.27
  30.3 0.1 broadcast_add_fusion
  30.4 0.1 fusion.17
  30.5 4.3 scatter_custom_fusion
  34.9 7.3 %gather_fusion = bf16[1152]{0:T(1024)(128)(2,1)S(1)} fusion(bf16[1025]{0:T(1024)(128)(2,1)S(1)} %pad_maximum_fusion.1, s32[2048]{0:T(1024)S(1)} %get-tuple-element.8), kind=kCustom, calls=%fused_computation | custom fusion | bytes 9216 | tf_op jit(solution)/shard_map/gather | solution.py:34
  42.2 0.8 all_to_all.16
  43.0 18.1 %all-to-all-start = ((bf16[64,1,18]{2,1,0:T(2,128)(2,1)}), bf16[64,1,18]{2,1,0:T(2,128)(2,1)S(1)}, u32[]{:S(2)}, u32[]{:S(2)}) async-start(bf16[64,1,18]{2,1,0:T(2,128)(2,1)} %all_to_all.16), calls=%async_computation | async-start | bytes 65536 | tf_op jit(solution)/shard_map/all_to_all | solution.py:37
  61.1 5.9 gather_fusion.2
  67.1 7.6 %reshape.386 = bf16[64,18,2048]{2,1,0:T(8,128)(2,1)} reshape(bf16[1152,2048]{1,0:T(8,128)(2,1)} %gather_fusion.2) | data formatting | bytes 9437184 | tf_op jit(solution)/shard_map/reshape | solution.py:32
  74.7 0.6 copy-done.7
  75.2 13.9 %all-to-all-start.2 = ((bf16[64,18,2048]{2,1,0:T(8,128)(2,1)}), bf16[64,18,2048]{2,1,0:T(8,128)(2,1)}, u32[]{:S(2)}, u32[]{:S(2)}) async-start(bf16[64,18,2048]{2,1,0:T(8,128)(2,1)} %reshape.386), calls=%async_computation.2 | async-start | bytes 12582912 | tf_op jit(solution)/shard_map/all_to_all | solution.py:36
  89.2 0.8 pad_maximum_fusion
  90.0 0.9 convert_reduce_fusion
  90.9 0.1 reshape.388
  91.1 0.9 fusion.8
  91.9 90.0 %all-gather.2.cloned.1.call-done = bf16[1,2,2048,384]{3,2,1,0:T(8,128)(2,1)} async-done(((bf16[1,2,256,384]{3,2,1,0:T(8,128)(2,1)}), bf16[1,2,2048,384]{3,2,1,0:T(8,128)(2,1)}) %all-gather.2.cloned.1.call-update) | async-done | bytes 3145744 | tf_op jit(solution)/shard_map/all_gather | solution.py:68
  182.0 4.2 fusion.12
  186.2 4.7 fusion
  190.9 7.6 %reshape_transpose_reshape.2 = bf16[64,18,2048]{2,1,0:T(8,128)(2,1)} reshape(bf16[1152,2048]{1,0:T(8,128)(2,1)} %fusion) | data formatting | bytes 9437184 | tf_op jit(solution)/shard_map/reshape;transpose;reshape | solution.py:75
  198.5 163.0 %all-to-all-done.2 = bf16[64,18,2048]{2,1,0:T(8,128)(2,1)} async-done(((bf16[64,18,2048]{2,1,0:T(8,128)(2,1)}), bf16[64,18,2048]{2,1,0:T(8,128)(2,1)}, u32[]{:S(2)}, u32[]{:S(2)}) %all-to-all-start.2) | async-done | bytes 4718624 | tf_op jit(solution)/shard_map/all_to_all | solution.py:36
  361.5 14.0 %all-to-all-start.1 = ((bf16[64,18,2048]{2,1,0:T(8,128)(2,1)}), bf16[64,18,2048]{2,1,0:T(8,128)(2,1)}, u32[]{:S(2)}, u32[]{:S(2)}) async-start(bf16[64,18,2048]{2,1,0:T(8,128)(2,1)} %reshape_transpose_reshape.2), calls=%async_computation.1 | async-start | bytes 12582912 | tf_op jit(solution)/shard_map/all_to_all | solution.py:77
  375.5 0.2 reduce-scatter.3.cloned.1.call-start
  375.7 7.7 %reshape.387 = bf16[1152,2048]{1,0:T(8,128)(2,1)} reshape(bf16[64,18,2048]{2,1,0:T(8,128)(2,1)} %all-to-all-done.2) | data formatting | bytes 9437184 | tf_op jit(solution)/shard_map/reshape.20
  383.4 6.3 fusion.1
  389.7 0.0 reduce-scatter.5.cloned.1.call-start
  389.8 6.5 fusion.2
  396.3 251.4 %all-to-all-done.1 = bf16[64,18,2048]{2,1,0:T(8,128)(2,1)} async-done(((bf16[64,18,2048]{2,1,0:T(8,128)(2,1)}), bf16[64,18,2048]{2,1,0:T(8,128)(2,1)}, u32[]{:S(2)}, u32[]{:S(2)}) %all-to-all-start.1) | async-done | bytes 4718624 | tf_op jit(solution)/shard_map/all_to_all | solution.py:77
  647.7 7.7 %reshape.384 = bf16[1152,2048]{1,0:T(8,128)(2,1)} reshape(bf16[64,18,2048]{2,1,0:T(8,128)(2,1)} %all-to-all-done.1) | data formatting | bytes 9437184 | tf_op jit(solution)/shard_map/reshape | solution.py:79
  655.4 5.2 concatenate.10
  660.6 11.8 %gather_fusion.1 = bf16[1024,2048]{1,0:T(8,128)(2,1)} fusion(bf16[1153,2048]{1,0:T(8,128)(2,1)} %concatenate.10, s32[1024]{0:T(1024)S(1)} %broadcast_clamp_fusion), kind=kCustom, calls=%fused_computation.1 | custom fusion | bytes 8392704 | tf_op jit(solution)/shard_map/gather | solution.py:82
  672.4 5.9 bitcast_reduce_fusion
  (32 shorter events, 0.3 us)
Async XLA Ops:
  34.9 26.2 %copy-start.4 = (bf16[128,2048]{1,0:T(8,128)(2,1)S(1)}, bf16[128,2048]{1,0:T(8,128)(2,1)}, u32[]{:S(2)}) copy-start(bf16[128,2048]{1,0:T(8,128)(2,1)} %param.9) | copy-start | bytes 1572868
  43.0 31.7 %all-to-all-start = ((bf16[64,1,18]{2,1,0:T(2,128)(2,1)}), bf16[64,1,18]{2,1,0:T(2,128)(2,1)S(1)}, u32[]{:S(2)}, u32[]{:S(2)}) async-start(bf16[64,1,18]{2,1,0:T(2,128)(2,1)} %all_to_all.16), calls=%async_computation | async-start | bytes 65536 | tf_op jit(solution)/shard_map/all_to_all | solution.py:37
  74.6 14.6 %copy-start.5 = (bf16[1,256,384]{2,1,0:T(8,128)(2,1)S(1)}, bf16[1,256,384]{2,1,0:T(8,128)(2,1)}, u32[]{:S(2)}) copy-start(bf16[1,256,384]{2,1,0:T(8,128)(2,1)} %param.17) | copy-start | bytes 589828
  74.6 14.6 %copy-start.6 = (bf16[1,256,384]{2,1,0:T(8,128)(2,1)S(1)}, bf16[1,256,384]{2,1,0:T(8,128)(2,1)}, u32[]{:S(2)}) copy-start(bf16[1,256,384]{2,1,0:T(8,128)(2,1)} %param.16) | copy-start | bytes 589828
  74.6 0.6 copy-start.7
  74.6 16.4 %copy-start.1 = (bf16[1,1,1152,384]{3,2,1,0:T(8,128)(2,1)S(1)}, bf16[1,1,1152,384]{3,2,1,0:T(8,128)(2,1)}, u32[]{:S(2)}) copy-start(bf16[1,1,1152,384]{3,2,1,0:T(8,128)(2,1)} %param.13) | copy-start | bytes 2654212
  74.7 16.4 %copy-start.2 = (bf16[1,1,1152,384]{3,2,1,0:T(8,128)(2,1)S(1)}, bf16[1,1,1152,384]{3,2,1,0:T(8,128)(2,1)}, u32[]{:S(2)}) copy-start(bf16[1,1,1152,384]{3,2,1,0:T(8,128)(2,1)} %param.14) | copy-start | bytes 2654212
  75.2 286.2 %all-to-all-start.2 = ((bf16[64,18,2048]{2,1,0:T(8,128)(2,1)}), bf16[64,18,2048]{2,1,0:T(8,128)(2,1)}, u32[]{:S(2)}, u32[]{:S(2)}) async-start(bf16[64,18,2048]{2,1,0:T(8,128)(2,1)} %reshape.386), calls=%async_computation.2 | async-start | bytes 12582912 | tf_op jit(solution)/shard_map/all_to_all | solution.py:36
  89.1 1.9 copy-start
  89.1 92.8 %all-gather.2.cloned.1.call-start = ((), (), s32[]{:S(2)}) async-start(), calls=%async_computation.5 | async-start | bytes 3538944 | tf_op jit(solution)/shard_map/all_gather | solution.py:68
  182.0 4.2 copy-start.3
  361.5 286.2 %all-to-all-start.1 = ((bf16[64,18,2048]{2,1,0:T(8,128)(2,1)}), bf16[64,18,2048]{2,1,0:T(8,128)(2,1)}, u32[]{:S(2)}, u32[]{:S(2)}) async-start(bf16[64,18,2048]{2,1,0:T(8,128)(2,1)} %reshape_transpose_reshape.2), calls=%async_computation.1 | async-start | bytes 12582912 | tf_op jit(solution)/shard_map/all_to_all | solution.py:77
  375.5 302.8 %reduce-scatter.3.cloned.1.call-start = ((), (), s32[]{:S(2)}) async-start(), calls=%async_computation.6 | async-start | bytes 1769472 | tf_op jit(solution)/shard_map/reduce_scatter | solution.py:61
  389.7 288.5 %reduce-scatter.5.cloned.1.call-start = ((), (), s32[]{:S(2)}) async-start(), calls=%async_computation.7 | async-start | bytes 1769472 | tf_op jit(solution)/shard_map/reduce_scatter | solution.py:64
Sparse Core Ops, SparseCore 0:
  93.8 88.1 all-gather.1
  389.9 89.3 reduce-scatter.2
  485.1 90.4 reduce-scatter.4
where the time goes:
time: 694 us; the launch traced here: 685 us
  waiting for transfers between devices  504 us (73%)
  local copies, waits for them, and re-layouts  70.2 us (10%)
  starting transfers between devices  46.2 us (7%)
  other arithmetic  28.1 us (4%)
  matrix products  21.7 us (3%)
  between operations  14 us (2%)
    all_to_all x1, waiting for transfers between devices, on_device(): lax.all_to_all(outgoing, 'expert', split_axis=0, concat_axis=0, tiled=True)  251 us
    all_to_all x1, waiting for transfers between devices, on_device(): lax.all_to_all(send_rows, 'expert', split_axis=0, concat_axis=0, tiled=True)  163 us
    all_gather x1, waiting for transfers between devices, on_device(): piece = lax.all_gather(stacked, 'dp', axis=2, tiled=True)  90 us
    another operation x3, other arithmetic  18.2 us
    all_to_all x1, starting transfers between devices, on_device(): lax.all_to_all(send_weights, 'expert', split_axis=0, concat_axis=0, tiled...  18.1 us
    all_to_all x1, starting transfers between devices, on_device(): lax.all_to_all(outgoing, 'expert', split_axis=0, concat_axis=0, tiled=True)  14 us
    all_to_all x1, starting transfers between devices, on_device(): lax.all_to_all(send_rows, 'expert', split_axis=0, concat_axis=0, tiled=True)  13.9 us
  transfers between devices with their start and end apart: 6, of which 3 were waited for; matrix products, arithmetic and copies ran while one was open for 12% of the time, Pallas kernels for 0%

commit v1 on v0

v1 whole, which is shorter than its diff:
```python
import functools

import jax
import jax.numpy as jnp
from jax import lax
from jax.experimental import pallas as pl
from jax.experimental.pallas import tpu as pltpu
from jax.sharding import PartitionSpec as P

MESH = pl.DeviceIdType.MESH
BF = jnp.bfloat16
F32 = jnp.float32
I32 = jnp.int32
PLANE = 4


def mm_nt(a, b):
    return lax.dot_general(a, b, (((1,), (1,)), ((), ())), preferred_element_type=F32)


def mm(a, b):
    return jnp.dot(a, b, preferred_element_type=F32)


def flip(bit, by):
    return bit + by - 2 * bit * by


def kernel(
    nz, ny, cap, topk,
    ids_in, keep_in, gate_in, tok, hid, pre_a, pre_b, w_gate, w_up,
    tok_out, gate_out, up_out,
    xcol, meta, delta, dperm, dturn, wall, st, xs_send, xs, g_send, g_all,
    fwd, bwd, tsum, part, prow, xsend, xrow,
    ag_s, ag_r, me_s, me_r, xd_s, xd_r, gd_s, gd_r, wx_s, wx_r, wy_s, wy_r,
    rs_s, rs_r, py_s, py_r, px_s, px_r,
):
    n2 = nz // 2
    tdev, width = tok.shape
    half = tdev // 2
    ff = w_gate.shape[1]
    rows = hid.shape[0]
    ch = n2 * cap
    db = w_gate.shape[0]
    nt = min(512, width)
    e_ix, d_ix = lax.axis_index("expert"), lax.axis_index("dp")
    z, q = e_ix // PLANE, e_ix % PLANE
    xl, co = q // 2, q % 2
    y, xh = d_ix // 2, d_ix % 2
    zup = (d_ix, lax.rem(z + 1, nz) * PLANE + q)
    zdn = (d_ix, lax.rem(z + nz - 1, nz) * PLANE + q)
    column = [flip(xl, r // 2) * 2 + flip(co, r % 2) for r in range(PLANE)]
    plane = [(d_ix, z * PLANE + column[r]) for r in range(PLANE)]
    ypeer = [(lax.rem(y + dy, ny) * 2 + xh, e_ix) for dy in range(ny)]
    xpeer = (y * 2 + (1 - xh), e_ix)

    def pos(off):
        if off == -n2 or off == n2:
            return nz - 1
        return 2 * off if off >= 0 else -2 * off - 1

    def send(src, dst, s, r, dev):
        return pltpu.make_async_remote_copy(
            src_ref=src, dst_ref=dst, send_sem=s, recv_sem=r, device_id=dev, device_id_type=MESH
        )

    def slot_half(p, h):
        return xcol.at[p // n2, pl.ds((p % n2) * tdev + h * half, half)]

    def ag_copy(way, d, h):
        sign = -1 if way == 0 else 1
        src = tok.at[pl.ds(h * half, half)] if d == 1 else slot_half(pos(sign * (d - 1)), h)
        ix = (way, d * 2 + h)
        return send(src, slot_half(pos(sign * d), h), ag_s.at[ix], ag_r.at[ix], zup if way == 0 else zdn)

    def me_copy(way, d):
        sign = -1 if way == 0 else 1
        ix = (way, d)
        return send(meta.at[pos(sign * (d - 1))], meta.at[pos(sign * d)], me_s.at[ix], me_r.at[ix], zup if way == 0 else zdn)

    def xd_copy(c, r):
        return send(xs_send.at[c, r - 1], xs.at[pl.ds((c * PLANE + r) * ch, ch)], xd_s.at[c, r], xd_r.at[c, r], plane[r])

    def gd_copy(c, r):
        return send(g_send.at[c, r - 1], g_all.at[c, pl.ds(r * ch, ch)], gd_s.at[c, r], gd_r.at[c, r], plane[r])

    def wblock(i):
        return wall.at[pl.ds(pl.multiple_of(i * db, db), db)]

    wx = send(wblock(d_ix), wblock(d_ix), wx_s, wx_r, xpeer)

    def wy_copy(dy, rel):
        i = y * 2 + flip(xh, rel)
        return send(wblock(i), wblock(i), wy_s.at[dy, rel], wy_r.at[dy, rel], ypeer[dy])

    def wy_wait(dy, rel):
        i = lax.rem(y + ny - dy, ny) * 2 + flip(xh, rel)
        send(wblock(i), wblock(i), wy_s.at[dy, rel], wy_r.at[dy, rel], ypeer[dy]).wait_recv()

    def rs_copy(way, d, h):
        buf = fwd if way == 0 else bwd
        ix = (way, d * 2 + h)
        return send(buf.at[d, h], buf.at[d - 1, h], rs_s.at[ix], rs_r.at[ix], zup if way == 0 else zdn)

    def py_copy(dy, rel):
        return send(part.at[dy, rel], prow.at[dy - 1, rel], py_s.at[dy, rel], py_r.at[dy, rel], ypeer[dy])

    px = send(xsend, xrow, px_s, px_r, xpeer)
    started = []

    def go(copy):
        copy.start()
        started.append(copy)

    barrier = pltpu.get_barrier_semaphore()
    partners = [zup, zdn, xpeer] + plane[1:] + ypeer[1:]
    for dev in partners:
        pl.semaphore_signal(barrier, inc=1, device_id=dev, device_id_type=MESH)

    experts = nz * PLANE
    ids, keep = ids_in[...], keep_in[...]
    e_iota = lax.broadcasted_iota(I32, (experts, tdev), 0)
    named = jnp.zeros((experts, tdev), F32)
    for k in range(topk):
        named += jnp.where((e_iota == ids[k:k + 1, :]) & (keep[k:k + 1, :] > 0), 1.0, 0.0)
    earlier = jnp.where(
        lax.broadcasted_iota(I32, (tdev, tdev), 0) < lax.broadcasted_iota(I32, (tdev, tdev), 1), 1.0, 0.0
    ).astype(BF)
    before = mm(named.astype(BF), earlier)
    for k in range(topk):
        mine = ids[k:k + 1, :]
        slot = jnp.sum(jnp.where(e_iota == mine, before, 0.0), axis=0, keepdims=True)
        row = mine.astype(F32) * float(cap) + slot
        meta[0, k:k + 1, :] = jnp.where(keep[k:k + 1, :] > 0, row, -4096.0)
    meta[0, topk:2 * topk, :] = gate_in[...]
    mine_w = pl.ds(pl.multiple_of(d_ix * db, db), db)
    wall[mine_w, 0:ff] = w_gate[...]
    wall[mine_w, ff:2 * ff] = w_up[...]

    pl.semaphore_wait(barrier, len(partners))

    def ag_has(way, d, h):
        return d < n2 or (d == n2 and h == way)

    def me_has(way, d):
        return d < n2 or (d == n2 and way == 0)

    for way in range(2):
        go(me_copy(way, 1))
    for h in range(2):
        for way in range(2):
            if ag_has(way, 1, h):
                go(ag_copy(way, 1, h))
    go(wx)
    for dy in range(1, ny):
        go(wy_copy(dy, 0))

    events = [(d, h) for d in range(1, n2) for h in range(2)] + [(n2, 0)]
    queue = list(events)

    def ag_event():
        if not queue:
            return
        d, h = queue.pop(0)
        for way in range(2):
            if h == 0 and me_has(way, d):
                me_copy(way, d).wait_recv()
                if me_has(way, d + 1):
                    go(me_copy(way, d + 1))
        for way in range(2):
            hh = way if d == n2 else h
            ag_copy(way, d, hh).wait_recv()
            if ag_has(way, d + 1, hh):
                go(ag_copy(way, d + 1, hh))

    tile = 96 if rows % 96 == 0 else rows
    tiles = rows // tile

    def delta_tile(i, _):
        at = pl.ds(pl.multiple_of(i * tile, tile), tile)
        a, b, dh = pre_a[at].astype(F32), pre_b[at].astype(F32), hid[at].astype(F32)
        s = 1.0 / (1.0 + jnp.exp(-a))
        delta[at, 0:ff] = (dh * b * s * (1.0 + a * (1.0 - s))).astype(BF)
        delta[at, ff:2 * ff] = (dh * a * s).astype(BF)
        return 0

    def perm_block(i, _):
        c, r = i // PLANE, i % PLANE
        other = flip(xl, r // 2) * 2 + flip(co, r % 2)
        rr = lax.broadcasted_iota(I32, (ch, 1), 0)
        m = jnp.zeros((ch, 1), I32)
        for k in range(1, n2):
            m += jnp.where(rr >= k * cap, 1, 0)
        p = m + c * n2
        low = p & 1
        off = jnp.where(low == 0, p >> 1, -((p + 1) >> 1))
        zz = off + z
        zz = jnp.where(zz < 0, zz + nz, zz)
        zz = jnp.where(zz >= nz, zz - nz, zz)
        want = zz * (PLANE * cap) + other * cap + rr - m * cap
        pick = jnp.where(lax.broadcasted_iota(I32, (ch, rows), 1) == want, 1.0, 0.0).astype(BF)
        dperm[pl.ds(pl.multiple_of(i * ch, ch), ch)] = mm(pick, delta[...]).astype(BF)
        return 0

    def turn_block(i, _):
        eye = jnp.where(
            lax.broadcasted_iota(I32, (128, 2 * ff), 0) + i * 128 == lax.broadcasted_iota(I32, (128, 2 * ff), 1), 1.0, 0.0
        ).astype(BF)
        dturn[pl.ds(pl.multiple_of(i * 128, 128), 128)] = mm_nt(eye, dperm[...]).astype(BF)
        return 0

    turns = 2 * ff // 128

    def pick_rows(p, r):
        base = ((z * PLANE + column[r]) * cap).astype(F32)
        v = meta[p, 0:topk, :] - base
        valid = (v >= 0.0) & (v < float(cap))
        row = jnp.max(jnp.where(valid, v + float((p % n2) * cap), -1.0), axis=0, keepdims=True)
        weight = jnp.sum(jnp.where(valid, meta[p, topk:2 * topk, :], 0.0), axis=0, keepdims=True)
        it = lax.broadcasted_iota(I32, (ch, tdev), 0).astype(F32)
        return jnp.where(it == row, weight, 0.0).astype(BF)

    eye_t = jnp.where(
        lax.broadcasted_iota(I32, (tdev, tdev), 0) == lax.broadcasted_iota(I32, (tdev, tdev), 1), 1.0, 0.0
    ).astype(BF)

    def combine_rows(p):
        s = jnp.concatenate([pick_rows(p, r) for r in range(PLANE)], axis=0)
        st[p] = mm_nt(eye_t, s).astype(BF)

    def select(c, r):
        s = jnp.concatenate([pick_rows(c * n2 + m, r) for m in range(n2)], axis=1)

        def body(i, _):
            at = pl.ds(pl.multiple_of(i * nt, nt), nt)
            got = mm(s, xcol[c, :, at]).astype(BF)
            if r == 0:
                xs[pl.ds(c * PLANE * ch, ch), at] = got
            else:
                xs_send[c, r - 1, :, at] = got
            return 0

        lax.fori_loop(0, width // nt, body, 0)
        if r:
            go(xd_copy(c, r))

    def slot_grads(c, r):
        lhs = dperm[pl.ds((c * PLANE + r) * ch, ch)]

        def body(i, _):
            at = pl.ds(pl.multiple_of(i * nt, nt), nt)
            got = mm_nt(lhs, wall[at]).astype(BF)
            if r == 0:
                g_all[c, 0:ch, at] = got
            else:
                g_send[c, r - 1, :, at] = got
            return 0

        lax.fori_loop(0, width // nt, body, 0)

    xcol[0, 0:tdev] = tok[...]
    split = tiles // 2
    lax.fori_loop(0, split, delta_tile, 0)
    lax.fori_loop(split, tiles, delta_tile, 0)
    ag_event()
    lax.fori_loop(PLANE, 2 * PLANE, perm_block, 0)
    ag_event()
    lax.fori_loop(0, PLANE, perm_block, 0)
    ag_event()
    wx_i = y * 2 + (1 - xh)
    send(wblock(wx_i), wblock(wx_i), wx_s, wx_r, xpeer).wait_recv()
    for dy in range(1, ny):
        go(wy_copy(dy, 1))
    lax.fori_loop(0, turns, turn_block, 0)
    near = n2 // 2

    def until(d, h):
        while queue and queue[0] <= (d, h):
            ag_event()

    until(n2 // 2, 1)
    for r in (2, 3):
        select(0, r)
    ag_event()
    for dy in range(1, ny):
        for rel in range(2):
            wy_wait(dy, rel)
    for r in (2, 3):
        slot_grads(1, r)
        go(gd_copy(1, r))
    ag_event()
    for r in (1, 0):
        slot_grads(1, r)
        if r:
            go(gd_copy(1, r))
    for r in (1, 0):
        select(0, r)
    ag_event()
    for r in (2, 3):
        slot_grads(0, r)
    ag_event()
    for r in (1, 0):
        slot_grads(0, r)
    for p in range(n2):
        combine_rows(p)
    ag_event()
    until(n2, 0)
    for r in (2, 3, 1, 0):
        select(1, r)
    for r in (2, 3, 1):
        go(gd_copy(0, r))
    for p in range(n2, nz):
        combine_rows(p)

    def rs_event(way, d, h):
        buf = fwd if way == 0 else bwd
        p = pos(d if way == 0 else -d)
        c = p // n2
        first = d == n2 or (d == n2 - 1 and h != way)
        lhs = st[p, h * half:(h + 1) * half]

        def body(i, _):
            at = pl.ds(pl.multiple_of(i * nt, nt), nt)
            tsum[way, :, at] = mm(lhs, g_all[c, :, at])
            return 0

        lax.fori_loop(0, width // nt, body, 0)
        if first:
            buf[d, h] = tsum[way].astype(BF)
        else:
            rs_copy(way, d + 1, h).wait_recv()
            buf[d, h] = (tsum[way] + buf[d, h].astype(F32)).astype(BF)
        go(rs_copy(way, d, h))

    def part_block(dy, rel):
        i = lax.rem(y + dy, ny) * 2 + flip(xh, rel)
        at = pl.ds(pl.multiple_of(i * db, db), db)
        part[dy, rel] = mm(dturn[...], xs[:, at]).astype(BF)
        if dy:
            go(py_copy(dy, rel))

    order = [(dy, rel) for dy in (2, 1, 3) if dy < ny for rel in (1, 0)] + [(0, 1), (0, 0)]
    g_waited = set()

    def need(c):
        if c not in g_waited:
            g_waited.add(c)
            for r in range(1, PLANE):
                gd_copy(c, r).wait_recv()

    steps = [(way, d, h) for d in range(n2, 0, -1) for h in range(2) for way in range(2) if d < n2 or h == way]
    waited_x = False
    for k, (way, d, h) in enumerate(steps):
        need(pos(d if way == 0 else -d) // n2)
        rs_event(way, d, h)
        if k >= min(6, len(steps) - 2) and k % 2 == 1:
            if not waited_x:
                waited_x = True
                for c in range(2):
                    for r in range(1, PLANE):
                        xd_copy(c, r).wait_recv()
            for _ in range(2):
                if order:
                    part_block(*order.pop(0))
    while order:
        part_block(*order.pop(0))

    def ysum(rel):
        total = part[0, rel].astype(F32)
        for dy in range(1, ny):
            total += prow[dy - 1, rel].astype(F32)
        return total

    for dy in range(1, ny):
        py_copy(dy, 1).wait_recv()
    xsend[...] = ysum(1).astype(BF)
    go(px)
    for h in range(2):
        lhs = st[0, h * half:(h + 1) * half]
        for n in range(width // nt):
            at = slice(n * nt, (n + 1) * nt)
            tsum[h, :, at] = mm(lhs, g_all[0, :, at])
    for dy in range(1, ny):
        py_copy(dy, 0).wait_recv()
    px.wait_recv()
    total = (ysum(0) + xrow[...].astype(F32)).astype(BF)
    eye_d = jnp.where(
        lax.broadcasted_iota(I32, (db, db), 0) == lax.broadcasted_iota(I32, (db, db), 1), 1.0, 0.0
    ).astype(BF)
    turned = mm_nt(eye_d, total).astype(BF)
    gate_out[...] = turned[:, 0:ff]
    up_out[...] = turned[:, ff:2 * ff]
    for h in range(2):
        for way in range(2):
            rs_copy(way, 1, h).wait_recv()
        tok_out[h * half:(h + 1) * half] = (tsum[h] + fwd[0, h].astype(F32) + bwd[0, h].astype(F32)).astype(BF)
    for copy in started:
        copy.wait_send()


def on_device(nz, ny, tokens, expert_ids, keep_mask, gate_weights, hidden_grad, gate_pre, up_pre, gate_proj, up_proj):
    tdev, width = tokens.shape
    topk = expert_ids.shape[1]
    rows, ff = hidden_grad.shape[2:]
    cap = rows // (nz * PLANE)
    n2 = nz // 2
    ch = n2 * cap
    db = gate_proj.shape[1]
    dma = pltpu.SemaphoreType.DMA
    vm = pl.BlockSpec(memory_space=pltpu.VMEM)
    grads = jax.ShapeDtypeStruct((db, ff), BF)
    out = pl.pallas_call(
        functools.partial(kernel, nz, ny, cap, topk),
        out_shape=(jax.ShapeDtypeStruct((tdev, width), BF), grads, grads),
        in_specs=[vm] * 9,
        out_specs=(vm, vm, vm),
        scratch_shapes=[
            pltpu.VMEM((2, n2 * tdev, width), BF),
            pltpu.VMEM((nz, 2 * topk, tdev), F32),
            pltpu.VMEM((rows, 2 * ff), BF),
            pltpu.VMEM((rows, 2 * ff), BF),
            pltpu.VMEM((2 * ff, rows), BF),
            pltpu.VMEM((width, 2 * ff), BF),
            pltpu.VMEM((nz, tdev, PLANE * ch), BF),
            pltpu.VMEM((2, PLANE - 1, ch, width), BF),
            pltpu.VMEM((rows, width), BF),
            pltpu.VMEM((2, PLANE - 1, ch, width), BF),
            pltpu.VMEM((2, PLANE * ch, width), BF),
            pltpu.VMEM((n2 + 1, 2, tdev // 2, width), BF),
            pltpu.VMEM((n2 + 1, 2, tdev // 2, width), BF),
            pltpu.VMEM((2, tdev // 2, width), F32),
            pltpu.VMEM((ny, 2, 2 * ff, db), BF),
            pltpu.VMEM((max(ny - 1, 1), 2, 2 * ff, db), BF),
            pltpu.VMEM((2 * ff, db), BF),
            pltpu.VMEM((2 * ff, db), BF),
            dma((2, 2 * n2 + 2)), dma((2, 2 * n2 + 2)),
            dma((2, n2 + 1)), dma((2, n2 + 1)),
            dma((2, PLANE)), dma((2, PLANE)),
            dma((2, PLANE)), dma((2, PLANE)),
            dma, dma,
            dma((ny, 2)), dma((ny, 2)),
            dma((2, 2 * n2 + 2)), dma((2, 2 * n2 + 2)),
            dma((ny, 2)), dma((ny, 2)),
            dma, dma,
        ],
        compiler_params=pltpu.CompilerParams(
            collective_id=0, has_side_effects=True, vmem_limit_bytes=61000 * 1024
        ),
        cost_estimate=pl.CostEstimate(
            flops=2 * rows * width * ff * 4, bytes_accessed=6 * rows * ff + 4 * tdev * width, transcendentals=rows * ff
        ),
    )(
        expert_ids.T, keep_mask.T, gate_weights.T.astype(F32), tokens,
        hidden_grad[0, 0], gate_pre[0, 0], up_pre[0, 0], gate_proj[0], up_proj[0],
    )
    return out[0], out[1][None], out[2][None]


def solution(mesh):
    nz, ny = mesh.shape["expert"] // PLANE, mesh.shape["dp"] // 2
    both = P(("dp", "expert"), None)
    acts = P("dp", "expert", None, None)
    weights = P("expert", "dp", None)
    return jax.shard_map(
        functools.partial(on_device, nz, ny),
        mesh=mesh,
        in_specs=(both, both, both, both, acts, acts, acts, weights, weights),
        out_specs=(both, weights, weights),
        check_vma=False,
    )
```

time: 694 us -> 219 us (0.32); the launches traced: 685 us -> 219 us
  waiting for transfers between devices: 504 us -> 0 us
  Pallas kernels: 0 us -> 214 us
  local copies, waits for them, and re-layouts: 70.2 us -> 4.27 us
  starting transfers between devices: 46.2 us -> 0 us
  other arithmetic: 28.1 us -> 0.59 us
  matrix products: 21.7 us -> 0 us
  between operations: 14 us -> 0.66 us
    all_to_all x3 -> x0, waiting for transfers between devices: 414 us -> none  [the longest x1 251 us: on_device(): lax.all_to_all(outgoing, 'expert', split_axis=0, concat_axis=0, tiled=True)]
    pallas_call x0 -> x1, Pallas kernels: none -> 214 us  [on_device(): pl.pallas_call(functools.partial(kernel, nz, ny, cap, topk), out_shape=(j...]
    all_gather x1 -> x0, waiting for transfers between devices: 90 us -> none  [on_device(): piece = lax.all_gather(stacked, 'dp', axis=2, tiled=True)]
    all_to_all x3 -> x0, starting transfers between devices: 45.9 us -> none  [the longest x1 18.1 us: on_device(): lax.all_to_all(send_weights, 'expert', split_axis=0, concat_axis=0, tiled...]
    gather x3 -> x0, local copies, waits for them, and re-layouts: 25 us -> none  [the longest x1 11.8 us: on_device(): picked = padded_grad[target].reshape(tok_rows, topk, width)]
    dot_general x4 -> x0, matrix products: 21.7 us -> none  [the longest x1 6.47 us: on_device(): jnp.einsum('erd,erf->edf', inputs_rx, up_delta, preferred_element_type=jn...]
    another operation x4 -> x0, other arithmetic: 19 us -> none
    another operation x4 -> x0, local copies, waits for them, and re-layouts: 15.4 us -> none
  transfers between devices with their start and end apart: 6 -> 0, of which waited for: 3 -> 0; matrix products, arithmetic and copies ran while one was open for 12% -> 0% of each run, Pallas kernels for 0% -> 0%
where the time goes in v1:
time: 219 us
  Pallas kernels  214 us (98%)
  local copies, waits for them, and re-layouts  4.27 us (2%)
    pallas_call x1, Pallas kernels, on_device(): pl.pallas_call(functools.partial(kernel, nz, ny, cap, topk), out_shape=(j...  214 us

profile of v1, /device:TPU:1, one launch (start us, length us, event | category | flops | bytes accessed | tf_op | source)
XLA Modules:
  0.0 219.1 jit_solution(12119583852482414618)
XLA Ops:
  0.6 0.0 copy-start.2
  0.6 0.7 copy-done.2
  1.3 0.6 convert_bitcast_fusion.gate_in
  1.9 213.5 %shard_map.112 = (bf16[128,2048]{1,0:T(8,128)(2,1)}, bf16[256,384]{1,0:T(8,128)(2,1)}, bf16[256,384]{1,0:T(8,128)(2,1)}) custom-call(s32[8,128]{1,0:T(8,128)} %bitcast.18, s32[8,128]{1,0:T(8,128)} %bitcast.19, f32[8,128]{1,0:T(8,128)} %convert_bitcast_fusion.gate_in, bf16[128,2048]{1,0:T(8,128)(2,1)} %tok.1, bf16[1152,384]{1,0:T(8,128)(2,1)} %bitcast.13, ...), custom_call_target="tpu_custom_call" | custom-call | flops 7247757312 | bytes 3702784 | tf_op jit(solution)/shard_map/pallas_call | solution.py:412
  215.4 0.0 copy-start.1
  215.5 1.9 copy.15
  217.4 0.0 copy-done.1
  217.4 0.0 copy-start
  217.4 0.7 copy.16
  218.1 0.3 copy-done
  218.4 0.7 copy.17
Async XLA Ops:
  0.6 0.7 copy-start.2
  215.4 1.9 copy-start.1
  217.4 1.0 copy-start

commit v2 on v1

--- a/solution.py
+++ b/solution.py
@@ -11,6 +11,8 @@
 BF = jnp.bfloat16
 F32 = jnp.float32
 I32 = jnp.int32
+NPA = 2
+NPR = 2
 PLANE = 4
 
 
@@ -37,10 +39,13 @@
 ):
     n2 = nz // 2
     tdev, width = tok.shape
-    half = tdev // 2
+    cut, rcut = tdev // NPA, tdev // NPR
     ff = w_gate.shape[1]
     rows = hid.shape[0]
     ch = n2 * cap
+    low = (n2 // 2) * cap // 16 * 16
+    span = ((0, low), (low, ch - low))
+    held = (range(0, -(-low // cap)), range(low // cap, n2))
     db = w_gate.shape[0]
     nt = min(512, width)
     e_ix, d_ix = lax.axis_index("expert"), lax.axis_index("dp")
@@ -64,25 +69,32 @@
             src_ref=src, dst_ref=dst, send_sem=s, recv_sem=r, device_id=dev, device_id_type=MESH
         )
 
-    def slot_half(p, h):
-        return xcol.at[p // n2, pl.ds((p % n2) * tdev + h * half, half)]
+    def slot_piece(p, h):
+        return xcol.at[p // n2, pl.ds((p % n2) * tdev + h * cut, cut)]
 
     def ag_copy(way, d, h):
         sign = -1 if way == 0 else 1
-        src = tok.at[pl.ds(h * half, half)] if d == 1 else slot_half(pos(sign * (d - 1)), h)
-        ix = (way, d * 2 + h)
-        return send(src, slot_half(pos(sign * d), h), ag_s.at[ix], ag_r.at[ix], zup if way == 0 else zdn)
+        src = tok.at[pl.ds(h * cut, cut)] if d == 1 else slot_piece(pos(sign * (d - 1)), h)
+        ix = (way, d * NPA + h)
+        return send(src, slot_piece(pos(sign * d), h), ag_s.at[ix], ag_r.at[ix], zup if way == 0 else zdn)
 
     def me_copy(way, d):
         sign = -1 if way == 0 else 1
         ix = (way, d)
         return send(meta.at[pos(sign * (d - 1))], meta.at[pos(sign * d)], me_s.at[ix], me_r.at[ix], zup if way == 0 else zdn)
 
-    def xd_copy(c, r):
-        return send(xs_send.at[c, r - 1], xs.at[pl.ds((c * PLANE + r) * ch, ch)], xd_s.at[c, r], xd_r.at[c, r], plane[r])
-
-    def gd_copy(c, r):
-        return send(g_send.at[c, r - 1], g_all.at[c, pl.ds(r * ch, ch)], gd_s.at[c, r], gd_r.at[c, r], plane[r])
+    def xd_copy(c, r, w):
+        at, n = span[w]
+        ix = (c * 2 + w, r)
+        return send(xs_send.at[c, r - 1, pl.ds(at, n)], xs.at[pl.ds((c * PLANE + r) * ch + at, n)], xd_s.at[ix], xd_r.at[ix], plane[r])
+
+    def g_rows(c, w):
+        return (c * ch + span[w][0]) * PLANE
+
+    def gd_copy(c, r, w):
+        at, n = span[w]
+        ix = (c * 2 + w, r)
+        return send(g_send.at[c, r - 1, pl.ds(at, n)], g_all.at[pl.ds(g_rows(c, w) + r * n, n)], gd_s.at[ix], gd_r.at[ix], plane[r])
 
     def wblock(i):
         return wall.at[pl.ds(pl.multiple_of(i * db, db), db)]
@@ -99,7 +111,7 @@
 
     def rs_copy(way, d, h):
         buf = fwd if way == 0 else bwd
-        ix = (way, d * 2 + h)
+        ix = (way, d * NPR + h)
         return send(buf.at[d, h], buf.at[d - 1, h], rs_s.at[ix], rs_r.at[ix], zup if way == 0 else zdn)
 
     def py_copy(dy, rel):
@@ -140,14 +152,14 @@
     pl.semaphore_wait(barrier, len(partners))
 
     def ag_has(way, d, h):
-        return d < n2 or (d == n2 and h == way)
+        return d < n2 or (d == n2 and h // (NPA // 2) == way)
 
     def me_has(way, d):
         return d < n2 or (d == n2 and way == 0)
 
     for way in range(2):
         go(me_copy(way, 1))
-    for h in range(2):
+    for h in range(NPA):
         for way in range(2):
             if ag_has(way, 1, h):
                 go(ag_copy(way, 1, h))
@@ -155,7 +167,7 @@
     for dy in range(1, ny):
         go(wy_copy(dy, 0))
 
-    events = [(d, h) for d in range(1, n2) for h in range(2)] + [(n2, 0)]
+    events = [(d, h) for d in range(1, n2) for h in range(NPA)] + [(n2, h) for h in range(NPA // 2)]
     queue = list(events)
 
     def ag_event():
@@ -163,12 +175,12 @@
             return
         d, h = queue.pop(0)
         for way in range(2):
-            if h == 0 and me_has(way, d):
+            if h == 0 and me_has(way, d) and d < n2:
                 me_copy(way, d).wait_recv()
                 if me_has(way, d + 1):
                     go(me_copy(way, d + 1))
         for way in range(2):
-            hh = way if d == n2 else h
+            hh = h + way * (NPA // 2) if d == n2 else h
             ag_copy(way, d, hh).wait_recv()
             if ag_has(way, d + 1, hh):
                 go(ag_copy(way, d + 1, hh))
@@ -211,117 +223,140 @@
 
     turns = 2 * ff // 128
 
-    def pick_rows(p, r):
+    def pick_rows(p, r, w):
         base = ((z * PLANE + column[r]) * cap).astype(F32)
         v = meta[p, 0:topk, :] - base
         valid = (v >= 0.0) & (v < float(cap))
-        row = jnp.max(jnp.where(valid, v + float((p % n2) * cap), -1.0), axis=0, keepdims=True)
+        row = jnp.max(jnp.where(valid, v + float((p % n2) * cap - span[w][0]), -1.0), axis=0, keepdims=True)
         weight = jnp.sum(jnp.where(valid, meta[p, topk:2 * topk, :], 0.0), axis=0, keepdims=True)
-        it = lax.broadcasted_iota(I32, (ch, tdev), 0).astype(F32)
+        it = lax.broadcasted_iota(I32, (span[w][1], tdev), 0).astype(F32)
         return jnp.where(it == row, weight, 0.0).astype(BF)
 
     eye_t = jnp.where(
         lax.broadcasted_iota(I32, (tdev, tdev), 0) == lax.broadcasted_iota(I32, (tdev, tdev), 1), 1.0, 0.0
     ).astype(BF)
 
+    def parts_of(p):
+        return [w for w in range(2) if p % n2 in held[w]]
+
+    def columns_of(w):
+        return slice(span[w][0] * PLANE, (span[w][0] + span[w][1]) * PLANE)
+
     def combine_rows(p):
-        s = jnp.concatenate([pick_rows(p, r) for r in range(PLANE)], axis=0)
-        st[p] = mm_nt(eye_t, s).astype(BF)
-
-    def select(c, r):
-        s = jnp.concatenate([pick_rows(c * n2 + m, r) for m in range(n2)], axis=1)
+        for w in parts_of(p):
+            s = jnp.concatenate([pick_rows(p, r, w) for r in range(PLANE)], axis=0)
+            st[p, :, columns_of(w)] = mm_nt(eye_t, s).astype(BF)
+
+    def combine(p, lo, n, at):
+        c = p // n2
+        total = None
+        for w in parts_of(p):
+            one = mm(st[p, lo:lo + n, columns_of(w)], g_all[pl.ds(g_rows(c, w), span[w][1] * PLANE), at])
+            total = one if total is None else total + one
+        return total
+
+    def select(c, r, w):
+        first, n = span[w]
+        s = jnp.concatenate([pick_rows(c * n2 + m, r, w) for m in held[w]], axis=1)
+        src = slice(held[w][0] * tdev, (held[w][-1] + 1) * tdev)
 
         def body(i, _):
             at = pl.ds(pl.multiple_of(i * nt, nt), nt)
-            got = mm(s, xcol[c, :, at]).astype(BF)
+            got = mm(s, xcol[c, src, at]).astype(BF)
             if r == 0:
-                xs[pl.ds(c * PLANE * ch, ch), at] = got
+                xs[pl.ds(c * PLANE * ch + first, n), at] = got
             else:
-                xs_send[c, r - 1, :, at] = got
+                xs_send[c, r - 1, first:first + n, at] = got
             return 0
 
         lax.fori_loop(0, width // nt, body, 0)
         if r:
-            go(xd_copy(c, r))
-
-    def slot_grads(c, r):
-        lhs = dperm[pl.ds((c * PLANE + r) * ch, ch)]
+            go(xd_copy(c, r, w))
+
+    def slot_grads(c, r, w):
+        first, n = span[w]
+        lhs = dperm[pl.ds((c * PLANE + r) * ch + first, n)]
 
         def body(i, _):
             at = pl.ds(pl.multiple_of(i * nt, nt), nt)
             got = mm_nt(lhs, wall[at]).astype(BF)
             if r == 0:
-                g_all[c, 0:ch, at] = got
+                g_all[pl.ds(g_rows(c, w), n), at] = got
             else:
-                g_send[c, r - 1, :, at] = got
+                g_send[c, r - 1, first:first + n, at] = got
             return 0
 
         lax.fori_loop(0, width // nt, body, 0)
 
+    def until(d, h):
+        while queue and queue[0] <= (d, h):
+            ag_event()
+
+    away = (2, 3, 1)
+
     xcol[0, 0:tdev] = tok[...]
-    split = tiles // 2
-    lax.fori_loop(0, split, delta_tile, 0)
-    lax.fori_loop(split, tiles, delta_tile, 0)
+    lax.fori_loop(0, tiles, delta_tile, 0)
     ag_event()
     lax.fori_loop(PLANE, 2 * PLANE, perm_block, 0)
-    ag_event()
-    lax.fori_loop(0, PLANE, perm_block, 0)
     ag_event()
     wx_i = y * 2 + (1 - xh)
     send(wblock(wx_i), wblock(wx_i), wx_s, wx_r, xpeer).wait_recv()
     for dy in range(1, ny):
         go(wy_copy(dy, 1))
+    lax.fori_loop(0, PLANE, perm_block, 0)
+    ag_event()
     lax.fori_loop(0, turns, turn_block, 0)
-    near = n2 // 2
-
-    def until(d, h):
-        while queue and queue[0] <= (d, h):
-            ag_event()
-
-    until(n2 // 2, 1)
-    for r in (2, 3):
-        select(0, r)
+    until((held[0][-1] + 1) // 2, NPA)
+    for r in away + (0,):
+        select(0, r, 0)
+    ag_event()
+    for p in range(n2 // 2):
+        combine_rows(p)
     ag_event()
     for dy in range(1, ny):
         for rel in range(2):
             wy_wait(dy, rel)
-    for r in (2, 3):
-        slot_grads(1, r)
-        go(gd_copy(1, r))
-    ag_event()
-    for r in (1, 0):
-        slot_grads(1, r)
-        if r:
-            go(gd_copy(1, r))
-    for r in (1, 0):
-        select(0, r)
-    ag_event()
-    for r in (2, 3):
-        slot_grads(0, r)
-    ag_event()
-    for r in (1, 0):
-        slot_grads(0, r)
-    for p in range(n2):
+    for r in away:
+        slot_grads(1, r, 1)
+        go(gd_copy(1, r, 1))
+    ag_event()
+    slot_grads(1, 0, 1)
+    until(n2 // 2, NPA)
+    for r in away:
+        select(0, r, 1)
+    for r in away:
+        slot_grads(1, r, 0)
+        go(gd_copy(1, r, 0))
+    ag_event()
+    select(0, 0, 1)
+    slot_grads(1, 0, 0)
+    for p in range(n2 // 2, n2):
         combine_rows(p)
     ag_event()
-    until(n2, 0)
-    for r in (2, 3, 1, 0):
-        select(1, r)
-    for r in (2, 3, 1):
-        go(gd_copy(0, r))
+    for r in range(PLANE):
+        slot_grads(0, r, 1)
+    ag_event()
+    until((n2 + held[0][-1] + 1) // 2, NPA)
+    for r in away + (0,):
+        select(1, r, 0)
+    ag_event()
+    for r in away:
+        go(gd_copy(0, r, 1))
+    for r in range(PLANE):
+        slot_grads(0, r, 0)
+    until(n2 - 1, NPA - 1)
+    me_copy(0, n2).wait_recv()
     for p in range(n2, nz):
         combine_rows(p)
 
     def rs_event(way, d, h):
         buf = fwd if way == 0 else bwd
         p = pos(d if way == 0 else -d)
-        c = p // n2
-        first = d == n2 or (d == n2 - 1 and h != way)
-        lhs = st[p, h * half:(h + 1) * half]
+        first = d == n2 or (d == n2 - 1 and h // (NPR // 2) != way)
 
         def body(i, _):
             at = pl.ds(pl.multiple_of(i * nt, nt), nt)
-            tsum[way, :, at] = mm(lhs, g_all[c, :, at])
+            tsum[way, :, at] = combine(p, h * rcut, rcut, at)
             return 0
 
         lax.fori_loop(0, width // nt, body, 0)
@@ -339,31 +374,30 @@
         if dy:
             go(py_copy(dy, rel))
 
-    order = [(dy, rel) for dy in (2, 1, 3) if dy < ny for rel in (1, 0)] + [(0, 1), (0, 0)]
     g_waited = set()
 
-    def need(c):
-        if c not in g_waited:
-            g_waited.add(c)
-            for r in range(1, PLANE):
-                gd_copy(c, r).wait_recv()
-
-    steps = [(way, d, h) for d in range(n2, 0, -1) for h in range(2) for way in range(2) if d < n2 or h == way]
-    waited_x = False
-    for k, (way, d, h) in enumerate(steps):
-        need(pos(d if way == 0 else -d) // n2)
-        rs_event(way, d, h)
-        if k >= min(6, len(steps) - 2) and k % 2 == 1:
-            if not waited_x:
-                waited_x = True
-                for c in range(2):
-                    for r in range(1, PLANE):
-                        xd_copy(c, r).wait_recv()
-            for _ in range(2):
-                if order:
-                    part_block(*order.pop(0))
-    while order:
-        part_block(*order.pop(0))
+    def need(p):
+        for w in parts_of(p):
+            if (p // n2, w) not in g_waited:
+                g_waited.add((p // n2, w))
+                for r in range(1, PLANE):
+                    gd_copy(p // n2, r, w).wait_recv()
+
+    far = [dy for dy in (2, 1, 3) if dy < ny]
+
+    def xd_wait():
+        for c in range(2):
+            for w in range(2):
+                for r in range(1, PLANE):
+                    xd_copy(c, r, w).wait_recv()
+
+    def parts_away(rel):
+        for dy in far:
+            part_block(dy, rel)
+
+    def parts_own():
+        for rel in (1, 0):
+            part_block(0, rel)
 
     def ysum(rel):
         total = part[0, rel].astype(F32)
@@ -371,15 +405,37 @@
             total += prow[dy - 1, rel].astype(F32)
         return total
 
-    for dy in range(1, ny):
-        py_copy(dy, 1).wait_recv()
-    xsend[...] = ysum(1).astype(BF)
-    go(px)
-    for h in range(2):
-        lhs = st[0, h * half:(h + 1) * half]
+    def cross():
+        for dy in range(1, ny):
+            py_copy(dy, 1).wait_recv()
+        xsend[...] = ysum(1).astype(BF)
+        go(px)
+
+    def last_rows():
+        until(n2, NPA)
+        for r in away + (0,):
+            select(1, r, 1)
+        for r in away:
+            go(gd_copy(0, r, 0))
+
+    steps = [(way, d, h) for d in range(n2, 0, -1) for h in range(NPR) for way in range(2) if d < n2 or h // (NPR // 2) == way]
+    pairs = len(steps) // 2
+    todo = [(1, last_rows), (pairs - 7, xd_wait), (pairs - 7, functools.partial(parts_away, 1)),
+            (pairs - 6, functools.partial(parts_away, 0)), (pairs - 5, parts_own), (pairs - 2, cross)]
+    for j in range(pairs):
+        for way, d, h in steps[2 * j:2 * j + 2]:
+            need(pos(d if way == 0 else -d))
+            rs_event(way, d, h)
+        while todo and todo[0][0] <= j:
+            todo.pop(0)[1]()
+    for _, what in todo:
+        what()
+
+    need(0)
+    for h in range(NPR):
         for n in range(width // nt):
             at = slice(n * nt, (n + 1) * nt)
-            tsum[h, :, at] = mm(lhs, g_all[0, :, at])
+            tsum[h, :, at] = combine(0, h * rcut, rcut, at)
     for dy in range(1, ny):
         py_copy(dy, 0).wait_recv()
     px.wait_recv()
@@ -390,10 +446,10 @@
     turned = mm_nt(eye_d, total).astype(BF)
     gate_out[...] = turned[:, 0:ff]
     up_out[...] = turned[:, ff:2 * ff]
-    for h in range(2):
+    for h in range(NPR):
         for way in range(2):
             rs_copy(way, 1, h).wait_recv()
-        tok_out[h * half:(h + 1) * half] = (tsum[h] + fwd[0, h].astype(F32) + bwd[0, h].astype(F32)).astype(BF)
+        tok_out[h * rcut:(h + 1) * rcut] = (tsum[h] + fwd[0, h].astype(F32) + bwd[0, h].astype(F32)).astype(BF)
     for copy in started:
         copy.wait_send()
 
@@ -425,21 +481,21 @@
             pltpu.VMEM((2, PLANE - 1, ch, width), BF),
             pltpu.VMEM((rows, width), BF),
             pltpu.VMEM((2, PLANE - 1, ch, width), BF),
-            pltpu.VMEM((2, PLANE * ch, width), BF),
-            pltpu.VMEM((n2 + 1, 2, tdev // 2, width), BF),
-            pltpu.VMEM((n2 + 1, 2, tdev // 2, width), BF),
-            pltpu.VMEM((2, tdev // 2, width), F32),
+            pltpu.VMEM((rows, width), BF),
+            pltpu.VMEM((n2 + 1, NPR, tdev // NPR, width), BF),
+            pltpu.VMEM((n2 + 1, NPR, tdev // NPR, width), BF),
+            pltpu.VMEM((NPR, tdev // NPR, width), F32),
             pltpu.VMEM((ny, 2, 2 * ff, db), BF),
             pltpu.VMEM((max(ny - 1, 1), 2, 2 * ff, db), BF),
             pltpu.VMEM((2 * ff, db), BF),
             pltpu.VMEM((2 * ff, db), BF),
-            dma((2, 2 * n2 + 2)), dma((2, 2 * n2 + 2)),
+            dma((2, NPA * (n2 + 1))), dma((2, NPA * (n2 + 1))),
             dma((2, n2 + 1)), dma((2, n2 + 1)),
-            dma((2, PLANE)), dma((2, PLANE)),
-            dma((2, PLANE)), dma((2, PLANE)),
+            dma((4, PLANE)), dma((4, PLANE)),
+            dma((4, PLANE)), dma((4, PLANE)),
             dma, dma,
             dma((ny, 2)), dma((ny, 2)),
-            dma((2, 2 * n2 + 2)), dma((2, 2 * n2 + 2)),
+            dma((2, NPR * (n2 + 1))), dma((2, NPR * (n2 + 1))),
             dma((ny, 2)), dma((ny, 2)),
             dma, dma,
         ],

time: 219 us -> 196 us (0.89)
  Pallas kernels: 214 us -> 190 us
    pallas_call x1, Pallas kernels: 214 us -> 190 us  [on_device(): pl.pallas_call(functools.partial(kernel, nz, ny, cap, topk), out_shape=(j...]
where the time goes in v2:
time: 196 us; the launch traced here: 195 us
  Pallas kernels  190 us (97%)
  local copies, waits for them, and re-layouts  4.27 us (2%)
    pallas_call x1, Pallas kernels, on_device(): pl.pallas_call(functools.partial(kernel, nz, ny, cap, topk), out_shape=(j...  190 us
    unnamed x9, local copies, waits for them, and re-layouts  4.27 us

profile of v2, /device:TPU:1, one launch (start us, length us, event | category | flops | bytes accessed | tf_op | source)
XLA Modules:
  0.0 195.1 jit_solution(4554059724470221116)
XLA Ops:
  0.6 0.0 copy-start.2
  0.6 0.7 copy-done.2
  1.3 0.6 convert_bitcast_fusion.gate_in
  1.9 189.6 %shard_map.112 = (bf16[128,2048]{1,0:T(8,128)(2,1)}, bf16[256,384]{1,0:T(8,128)(2,1)}, bf16[256,384]{1,0:T(8,128)(2,1)}) custom-call(s32[8,128]{1,0:T(8,128)} %bitcast.18, s32[8,128]{1,0:T(8,128)} %bitcast.19, f32[8,128]{1,0:T(8,128)} %convert_bitcast_fusion.gate_in, bf16[128,2048]{1,0:T(8,128)(2,1)} %tok.1, bf16[1152,384]{1,0:T(8,128)(2,1)} %bitcast.13, ...), custom_call_target="tpu_custom_call" | custom-call | flops 7247757312 | bytes 3702784 | tf_op jit(solution)/shard_map/pallas_call | solution.py:468
  191.5 0.0 copy-start.1
  191.5 1.9 copy.15
  193.5 0.0 copy-done.1
  193.5 0.0 copy-start
  193.5 0.7 copy.16
  194.1 0.3 copy-done
  194.5 0.7 copy.17
Async XLA Ops:
  0.6 0.7 copy-start.2
  191.5 1.9 copy-start.1
  193.5 1.0 copy-start

commit v3 on v2

--- a/solution.py
+++ b/solution.py
@@ -30,12 +30,12 @@
 
 def kernel(
     nz, ny, cap, topk,
-    ids_in, keep_in, gate_in, tok, hid, pre_a, pre_b, w_gate, w_up,
+    ids_in, keep_in, gate_in, tok, hid_in, pre_a_in, pre_b_in, w_gate, w_up,
     tok_out, gate_out, up_out,
     xcol, meta, delta, dperm, dturn, wall, st, xs_send, xs, g_send, g_all,
     fwd, bwd, tsum, part, prow, xsend, xrow,
     ag_s, ag_r, me_s, me_r, xd_s, xd_r, gd_s, gd_r, wx_s, wx_r, wy_s, wy_r,
-    rs_s, rs_r, py_s, py_r, px_s, px_r,
+    rs_s, rs_r, py_s, py_r, px_s, px_r, hid, pre_a, pre_b, in_s,
 ):
     n2 = nz // 2
     tdev, width = tok.shape
@@ -74,7 +74,7 @@
 
     def ag_copy(way, d, h):
         sign = -1 if way == 0 else 1
-        src = tok.at[pl.ds(h * cut, cut)] if d == 1 else slot_piece(pos(sign * (d - 1)), h)
+        src = slot_piece(pos(sign * (d - 1)), h)
         ix = (way, d * NPA + h)
         return send(src, slot_piece(pos(sign * d), h), ag_s.at[ix], ag_r.at[ix], zup if way == 0 else zdn)
 
@@ -128,6 +128,20 @@
     partners = [zup, zdn, xpeer] + plane[1:] + ypeer[1:]
     for dev in partners:
         pl.semaphore_signal(barrier, inc=1, device_id=dev, device_id_type=MESH)
+
+    mine_w = pl.ds(pl.multiple_of(d_ix * db, db), db)
+    fetch_w = [
+        pltpu.make_async_copy(w_gate, wall.at[mine_w, pl.ds(0, ff)], in_s.at[0]),
+        pltpu.make_async_copy(w_up, wall.at[mine_w, pl.ds(ff, ff)], in_s.at[1]),
+    ]
+    fetch = [
+        pltpu.make_async_copy(hid_in, hid, in_s.at[2]),
+        pltpu.make_async_copy(pre_a_in, pre_a, in_s.at[3]),
+        pltpu.make_async_copy(pre_b_in, pre_b, in_s.at[4]),
+        pltpu.make_async_copy(tok, xcol.at[0, pl.ds(0, tdev)], in_s.at[5]),
+    ]
+    for copy in fetch[3:] + fetch_w + fetch[:3]:
+        copy.start()
 
     experts = nz * PLANE
     ids, keep = ids_in[...], keep_in[...]
@@ -144,10 +158,7 @@
         slot = jnp.sum(jnp.where(e_iota == mine, before, 0.0), axis=0, keepdims=True)
         row = mine.astype(F32) * float(cap) + slot
         meta[0, k:k + 1, :] = jnp.where(keep[k:k + 1, :] > 0, row, -4096.0)
-    meta[0, topk:2 * topk, :] = gate_in[...]
-    mine_w = pl.ds(pl.multiple_of(d_ix * db, db), db)
-    wall[mine_w, 0:ff] = w_gate[...]
-    wall[mine_w, ff:2 * ff] = w_up[...]
+    meta[0, topk:2 * topk, :] = gate_in[...].astype(F32)
 
     pl.semaphore_wait(barrier, len(partners))
 
@@ -157,12 +168,15 @@
     def me_has(way, d):
         return d < n2 or (d == n2 and way == 0)
 
+    fetch[3].wait()
     for way in range(2):
         go(me_copy(way, 1))
     for h in range(NPA):
         for way in range(2):
             if ag_has(way, 1, h):
                 go(ag_copy(way, 1, h))
+    for copy in fetch_w:
+        copy.wait()
     go(wx)
     for dy in range(1, ny):
         go(wy_copy(dy, 0))
@@ -294,7 +308,8 @@
 
     away = (2, 3, 1)
 
-    xcol[0, 0:tdev] = tok[...]
+    for copy in fetch[:3]:
+        copy.wait()
     lax.fori_loop(0, tiles, delta_tile, 0)
     ag_event()
     lax.fori_loop(PLANE, 2 * PLANE, perm_block, 0)
@@ -454,6 +469,12 @@
         copy.wait_send()
 
 
+def hand_on(tok, gate, up, tok_out, gate_out, up_out):
+    tok_out[...] = tok[...]
+    gate_out[0] = gate[...]
+    up_out[0] = up[...]
+
+
 def on_device(nz, ny, tokens, expert_ids, keep_mask, gate_weights, hidden_grad, gate_pre, up_pre, gate_proj, up_proj):
     tdev, width = tokens.shape
     topk = expert_ids.shape[1]
@@ -464,11 +485,12 @@
     db = gate_proj.shape[1]
     dma = pltpu.SemaphoreType.DMA
     vm = pl.BlockSpec(memory_space=pltpu.VMEM)
+    hbm = pl.BlockSpec(memory_space=pl.ANY)
     grads = jax.ShapeDtypeStruct((db, ff), BF)
     out = pl.pallas_call(
         functools.partial(kernel, nz, ny, cap, topk),
         out_shape=(jax.ShapeDtypeStruct((tdev, width), BF), grads, grads),
-        in_specs=[vm] * 9,
+        in_specs=[vm] * 3 + [hbm] * 6,
         out_specs=(vm, vm, vm),
         scratch_shapes=[
             pltpu.VMEM((2, n2 * tdev, width), BF),
@@ -498,6 +520,10 @@
             dma((2, NPR * (n2 + 1))), dma((2, NPR * (n2 + 1))),
             dma((ny, 2)), dma((ny, 2)),
             dma, dma,
+            pltpu.VMEM((rows, ff), BF),
+            pltpu.VMEM((rows, ff), BF),
+            pltpu.VMEM((rows, ff), BF),
+            dma((6,)),
         ],
         compiler_params=pltpu.CompilerParams(
             collective_id=0, has_side_effects=True, vmem_limit_bytes=61000 * 1024
@@ -506,10 +532,17 @@
             flops=2 * rows * width * ff * 4, bytes_accessed=6 * rows * ff + 4 * tdev * width, transcendentals=rows * ff
         ),
     )(
-        expert_ids.T, keep_mask.T, gate_weights.T.astype(F32), tokens,
+        expert_ids.T, keep_mask.T, gate_weights.T, tokens,
         hidden_grad[0, 0], gate_pre[0, 0], up_pre[0, 0], gate_proj[0], up_proj[0],
     )
-    return out[0], out[1][None], out[2][None]
+    whole = jax.ShapeDtypeStruct((1, db, ff), BF)
+    return pl.pallas_call(
+        hand_on,
+        out_shape=(jax.ShapeDtypeStruct((tdev, width), BF), whole, whole),
+        in_specs=[vm] * 3,
+        out_specs=(vm, vm, vm),
+        cost_estimate=pl.CostEstimate(flops=0, bytes_accessed=4 * (tdev * width + 2 * db * ff), transcendentals=0),
+    )(*out)
 
 
 def solution(mesh):

time: 196 us -> 192 us (0.980)
  local copies, waits for them, and re-layouts: 4.27 us -> 0 us
    unnamed x9 -> x0, local copies, waits for them, and re-layouts: 4.27 us -> none
    pallas_call x0 -> x1, Pallas kernels: none -> 2.12 us  [on_device(): pl.pallas_call(hand_on, out_shape=(jax.ShapeDtypeStruct((tdev, width), BF...]
where the time goes in v3:
time: 192 us; the launch traced here: 191 us
  Pallas kernels  191 us (99%)
    pallas_call x1, Pallas kernels, on_device(): pl.pallas_call(functools.partial(kernel, nz, ny, cap, topk), out_shape=(j...  188 us

profile of v3, /device:TPU:1, one launch (start us, length us, event | category | flops | bytes accessed | tf_op | source)
XLA Modules:
  0.0 191.2 jit_solution(14495969771728772355)
XLA Ops:
  0.6 188.4 %shard_map.112 = (bf16[128,2048]{1,0:T(8,128)(2,1)}, bf16[256,384]{1,0:T(8,128)(2,1)}, bf16[256,384]{1,0:T(8,128)(2,1)}) custom-call(s32[8,128]{1,0:T(8,128)} %bitcast.13, s32[8,128]{1,0:T(8,128)} %bitcast.14, bf16[8,128]{1,0:T(8,128)(2,1)} %bitcast.15, bf16[128,2048]{1,0:T(8,128)(2,1)} %tok.1, bf16[1152,384]{1,0:T(8,128)(2,1)} %bitcast.8, ...), custom_call_target="tpu_custom_call" | custom-call | flops 7247757312 | bytes 3702784 | tf_op jit(solution)/shard_map/pallas_call | solution.py:490
  189.0 2.1 %shard_map.113 = (bf16[128,2048]{1,0:T(8,128)(2,1)}, bf16[1,256,384]{2,1,0:T(8,128)(2,1)}, bf16[1,256,384]{2,1,0:T(8,128)(2,1)}) custom-call(bf16[128,2048]{1,0:T(8,128)(2,1)} %get-tuple-element.6.tok, bf16[256,384]{1,0:T(8,128)(2,1)} %get-tuple-element.7.gate, bf16[256,384]{1,0:T(8,128)(2,1)} %get-tuple-element.8.up), custom_call_target="tpu_custom_call" | custom-call | bytes 1835008 | tf_op jit(solution)/shard_map/pallas_call | solution.py:539

commit v4 on v3

--- a/solution.py
+++ b/solution.py
@@ -143,6 +143,19 @@
     for copy in fetch[3:] + fetch_w + fetch[:3]:
         copy.start()
 
+    pl.semaphore_wait(barrier, len(partners))
+
+    def ag_has(way, d, h):
+        return d < n2 or (d == n2 and h // (NPA // 2) == way)
+
+    def me_has(way, d):
+        return d < n2 or (d == n2 and way == 0)
+
+    fetch[3].wait()
+    for way in range(2):
+        if ag_has(way, 1, 0):
+            go(ag_copy(way, 1, 0))
+
     experts = nz * PLANE
     ids, keep = ids_in[...], keep_in[...]
     e_iota = lax.broadcasted_iota(I32, (experts, tdev), 0)
@@ -160,18 +173,9 @@
         meta[0, k:k + 1, :] = jnp.where(keep[k:k + 1, :] > 0, row, -4096.0)
     meta[0, topk:2 * topk, :] = gate_in[...].astype(F32)
 
-    pl.semaphore_wait(barrier, len(partners))
-
-    def ag_has(way, d, h):
-        return d < n2 or (d == n2 and h // (NPA // 2) == way)
-
-    def me_has(way, d):
-        return d < n2 or (d == n2 and way == 0)
-
-    fetch[3].wait()
     for way in range(2):
         go(me_copy(way, 1))
-    for h in range(NPA):
+    for h in range(1, NPA):
         for way in range(2):
             if ag_has(way, 1, h):
                 go(ag_copy(way, 1, h))

time: 192 us -> 192 us (level)
  no operation moved by 1% of the time
where the time goes in v4:
time: 192 us; the launch traced here: 191 us
  Pallas kernels  191 us (99%)
    pallas_call x1, Pallas kernels, on_device(): pl.pallas_call(functools.partial(kernel, nz, ny, cap, topk), out_shape=(j...  188 us

profile of v4, /device:TPU:1, one launch (start us, length us, event | category | flops | bytes accessed | tf_op | source)
XLA Modules:
  0.0 191.2 jit_solution(13281477993668545510)
XLA Ops:
  0.6 188.4 %shard_map.112 = (bf16[128,2048]{1,0:T(8,128)(2,1)}, bf16[256,384]{1,0:T(8,128)(2,1)}, bf16[256,384]{1,0:T(8,128)(2,1)}) custom-call(s32[8,128]{1,0:T(8,128)} %bitcast.13, s32[8,128]{1,0:T(8,128)} %bitcast.14, bf16[8,128]{1,0:T(8,128)(2,1)} %bitcast.15, bf16[128,2048]{1,0:T(8,128)(2,1)} %tok.1, bf16[1152,384]{1,0:T(8,128)(2,1)} %bitcast.8, ...), custom_call_target="tpu_custom_call" | custom-call | flops 7247757312 | bytes 3702784 | tf_op jit(solution)/shard_map/pallas_call | solution.py:494
  189.1 2.1 %shard_map.113 = (bf16[128,2048]{1,0:T(8,128)(2,1)}, bf16[1,256,384]{2,1,0:T(8,128)(2,1)}, bf16[1,256,384]{2,1,0:T(8,128)(2,1)}) custom-call(bf16[128,2048]{1,0:T(8,128)(2,1)} %get-tuple-element.6.tok, bf16[256,384]{1,0:T(8,128)(2,1)} %get-tuple-element.7.gate, bf16[256,384]{1,0:T(8,128)(2,1)} %get-tuple-element.8.up), custom_call_target="tpu_custom_call" | custom-call | bytes 1835008 | tf_op jit(solution)/shard_map/pallas_call | solution.py:543
